TPU v7x, 256 devices: a whole 4x4x8 slice. The times are simulated.
256 devices in a mesh: panel: 64 (over y, x, z_lo), slab: 4 (over z_hi, core).
Axes of the slice: x: 4, y: 4, z: 8 (z_hi: 2, z_lo: 4; z = z_hi * 4 + z_lo), core: 2. Of those that a mesh axis runs over, the one named last changes fastest.
Arguments:
- clip_cache: float32 [1024, 8192], P(None, 'panel'), may hold values from -6 to 6
- dose_scale: float32 [16, 8192], P(None, 'panel'), may hold values from 0.3 to 3
- focus_term: float32 [8, 8192], P(None, 'panel'), may hold values from -3 to 3
- clip_ids: int32 [32768], P('slab'), may hold values from 0 to 1023
- dose_ids: int32 [32768], P('slab'), may hold values from 0 to 15
- focus_ids: int32 [32768], P('slab'), may hold values from 0 to 7
Outputs:
- rotated: float32 [32768, 8192], P('slab', 'panel')
All inputs are finite; a program needn't handle non-finite values.
Results may differ from a plain program's by a relative error of at most 0.0001.
Values sent between devices are 32-bit elements; how exact they have to be, the bound alone decides.
A program may use at most 64 MiB of HBM per device.

v0:
```python
import jax
import jax.numpy as jnp
from jax import lax
from jax.sharding import PartitionSpec as P

ROUNDS = 2
EPSILON = 1e-06


def from_behind(block, axis, distance):
    devices = range(lax.axis_size(axis))
    route = [((i - distance) % len(devices), i) for i in devices]
    return lax.ppermute(block, axis, route)


def from_partner(value, axis, distance):
    mask = 2**distance
    pairs = [(source, source ^ mask) for source in range(lax.axis_size(axis))]
    return lax.ppermute(value, axis, pairs)


def block_rotation(gram):
    doubled = gram.shape[0]
    half_size = doubled // 2
    diagonal = jnp.diagonal(gram)
    coupling = gram / (diagonal[:, None] + diagonal[None, :])
    positions = lax.iota(jnp.int32, doubled)
    upper_mask = (positions[:, None] < half_size) & (positions[None, :] >= half_size)
    lower_mask = (positions[:, None] >= half_size) & (positions[None, :] < half_size)
    generator = 0.5 * (jnp.where(upper_mask, coupling, 0.0) - jnp.where(lower_mask, coupling, 0.0))
    identity = jnp.eye(doubled, dtype=gram.dtype)
    plus_half = identity + generator
    symmetric = identity + jnp.dot(
        generator.T, generator, precision=lax.Precision.HIGHEST, preferred_element_type=jnp.float32
    )
    factor = jnp.linalg.cholesky(symmetric)
    numerator = jnp.dot(
        plus_half, plus_half, precision=lax.Precision.HIGHEST, preferred_element_type=jnp.float32
    )
    return jax.scipy.linalg.cho_solve((factor, True), numerator)


def lookup(table_rows, indices):
    positions = lax.iota(jnp.int32, table_rows.shape[0])
    one_hot = (positions[:, None] == indices[None, :]).astype(jnp.float32)
    return lax.dot_general(
        one_hot,
        table_rows,
        (((0,), (0,)), ((), ())),
        precision=lax.Precision.HIGHEST,
        preferred_element_type=jnp.float32,
    )


def slab_gram(pair_block):
    gram_local = lax.dot_general(
        pair_block,
        pair_block,
        (((0,), (0,)), ((), ())),
        precision=lax.Precision.HIGHEST,
        preferred_element_type=jnp.float32,
    )
    return lax.psum(gram_local, "slab")


def product(left_side, right_side):
    return jnp.dot(
        left_side, right_side, precision=lax.Precision.HIGHEST, preferred_element_type=jnp.float32
    )


def shards(clip_cache, dose_scale, focus_term, clip_ids, dose_ids, focus_ids):
    row_count = clip_ids.shape[0]
    total_rows = row_count * lax.axis_size("slab")
    panel_width = clip_cache.shape[1]
    dose_part = lookup(dose_scale, dose_ids)
    focus_part = lookup(focus_term, focus_ids)
    jacobian = jnp.take(clip_cache, clip_ids, axis=0) * dose_part + focus_part
    col_squares = lax.psum(jnp.sum(jacobian * jacobian, axis=0), "slab")
    jacobian = jacobian * (1.0 / jnp.sqrt(col_squares / total_rows + EPSILON))
    seat_index = lax.axis_index("panel")
    is_odd = seat_index % 2 == 1
    own_start = seat_index % 2 * panel_width
    current = jacobian
    for section in range(ROUNDS):
        if section > 0:
            current = from_behind(current, "panel", 1)
        partner = from_partner(current, "panel", 0)
        pair_block = jnp.where(
            is_odd,
            jnp.concatenate([partner, current], axis=1),
            jnp.concatenate([current, partner], axis=1),
        )
        rotation = block_rotation(slab_gram(pair_block))
        own_cols = lax.dynamic_slice_in_dim(rotation, own_start, panel_width, 1)
        current = product(pair_block, own_cols)
    return current


def solution(mesh):
    return jax.shard_map(
        shards,
        mesh=mesh,
        in_specs=(
            P(None, "panel"),
            P(None, "panel"),
            P(None, "panel"),
            P("slab"),
            P("slab"),
            P("slab"),
        ),
        out_specs=P("slab", "panel"),
        check_vma=False,
    )
```

profile of v0, /device:TPU:1, one launch (start us, length us, event | category | flops | bytes accessed | tf_op | source)
XLA Modules:
  0.0 656.2 jit_solution(8444615578186647330)
XLA Ops:
  6.5 0.8 fusion.42
  7.4 0.8 compare_and_fusion
  8.2 28.0 %gather_fusion = f32[8192,128]{1,0:T(8,128)} fusion(f32[1024,128]{1,0:T(8,128)S(1)} %copy-done, s32[8192]{0:T(1024)S(1)} %fusion.42), kind=kCustom, calls=%fused_computation | custom fusion | bytes 8421376 | tf_op jit(solution)/shard_map/jit(_take)/gather | solution.py:78
  36.1 5.7 copy.15
  41.8 4.2 convolution_multiply_fusion
  46.0 4.2 multiply_reduce_fusion
  50.2 12.1 %psum.21 = f32[128]{0:T(128)S(1)} all-reduce(f32[128]{0:T(128)S(1)} %get-tuple-element.51), channel_id=1, replica_groups=mesh['panel'=64,'slab'=4] {'slab'}, use_global_device_ids=true, to_apply=%region_1.2 | all-reduce | flops 128 | bytes 1024 | tf_op jit(solution)/shard_map/psum | solution.py:79
  62.3 4.7 broadcast_multiply_fusion
  67.0 0.7 collective-permute-start
  67.7 85.9 %collective-permute-done = f32[8192,128]{0,1:T(8,128)} collective-permute-done((f32[8192,128]{0,1:T(8,128)}, f32[8192,128]{0,1:T(8,128)}, u32[]{:S(2)}, u32[]{:S(2)}) %collective-permute-start) | collective-permute-done | bytes 4194336 | tf_op jit(solution)/shard_map/ppermute | solution.py:19
  153.5 15.8 %fusion.3 = f32[256,256]{0,1:T(8,128)} fusion(f32[8192,128]{0,1:T(8,128)} %broadcast_multiply_fusion, f32[8192,128]{0,1:T(8,128)} %collective-permute-done, pred[]{:T(512)S(6)} %eq.42), kind=kOutput, calls=%fused_computation.14 | convolution fusion | flops 6448742400 | bytes 8650753 | tf_op jit(solution)/shard_map/dot_general | solution.py:56
  169.4 0.2 all-reduce.6.cloned.1.call-start
  169.6 62.4 %all-reduce.4.cloned.1.call-done = f32[256,256]{0,1:T(8,128)} async-done(((f32[256,256]{0,1:T(8,128)}), f32[256,256]{0,1:T(8,128)}) %all-reduce.4.cloned.1.call-update) | async-done | bytes 262160 | tf_op jit(solution)/shard_map/psum | solution.py:63
  232.0 2.7 gather_fusion.1
  234.7 1.6 convolution_add_fusion.2
  236.5 11.7 %cholesky.130 = f32[128,128]{1,0:T(8,128)S(1)} custom-call(f32[128,128]{1,0:T(8,128)S(1)} %cholesky.194), custom_call_target="Cholesky" | custom-call | tf_op jit(solution)/shard_map/jit(cholesky)/cholesky | solution.py:36
  248.3 9.8 %custom-call.19 = f32[1,128,128]{1,2,0:T(8,128)S(1)} custom-call(f32[1,128,128]{2,1,0:T(8,128)S(1)} %get-tuple-element.50), custom_call_target="InvertDiagBlocksLowerTriangular" | custom-call | tf_op jit(solution)/shard_map/jit(cholesky)/cholesky | solution.py:36
  258.1 0.2 constant_dynamic-update-slice_fusion.1
  258.3 0.3 convolution_subtract_fusion.5
  258.6 11.7 %cholesky.147 = f32[128,128]{1,0:T(8,128)S(1)} custom-call(f32[128,128]{1,0:T(8,128)S(1)} %convolution_subtract_fusion.5), custom_call_target="Cholesky" | custom-call | tf_op jit(solution)/shard_map/jit(cholesky)/cholesky | solution.py:36
  270.3 0.7 compare_reduce_fusion.2
  271.1 0.6 compare_reduce_fusion.3
  273.1 4.2 while.4
  273.3 0.6 fusion.73
  273.9 1.4 bitcast_dynamic-update-slice_fusion.4
  275.3 0.6 fusion.73
  275.9 1.4 bitcast_dynamic-update-slice_fusion.4
  277.3 19.7 %custom-call.20 = f32[2,128,128]{1,2,0:T(8,128)S(1)} custom-call(f32[2,128,128]{2,1,0:T(8,128)S(1)} %get-tuple-element.21), custom_call_target="InvertDiagBlocksLowerTriangular" | custom-call | tf_op jit(solution)/shard_map/jit(_cho_solve)/triangular_solve | solution.py:40
  297.0 0.8 fusion.12
  297.8 0.3 fusion.23
  298.1 0.3 convolution_subtract_fusion.3
  298.4 0.3 fusion.34
  298.7 0.3 fusion.33
  299.0 0.3 convolution_subtract_fusion.2
  299.3 0.3 fusion.32
  299.6 8.8 %fusion.2 = f32[8192,128]{0,1:T(8,128)S(1)} fusion(f32[8192,128]{0,1:T(8,128)} %broadcast_multiply_fusion, f32[8192,128]{0,1:T(8,128)} %collective-permute-done, pred[]{:T(512)S(6)} %eq.42, s32[]{:T(128)S(6)} %select_n.63, f32[128,256]{1,0:T(8,128)S(1)} %fusion.32, f32[128,256]{1,0:T(8,128)S(1)} %fusion.33), kind=kOutput, calls=%fused_computation.13 | convolution fusion | flops 3227549696 | bytes 12845061 | tf_op jit(solution)/shard_map/dot_general | solution.py:67
  308.4 98.5 %collective-permute-done.1 = f32[8192,128]{0,1:T(8,128)S(1)} collective-permute-done((f32[8192,128]{0,1:T(8,128)S(1)}, f32[8192,128]{0,1:T(8,128)S(1)}, u32[]{:S(2)}, u32[]{:S(2)}) %collective-permute-start.1) | collective-permute-done | bytes 4194336 | tf_op jit(solution)/shard_map/ppermute | solution.py:13
  406.9 1.9 copy-done.7
  408.8 91.7 %collective-permute-done.2 = f32[8192,128]{0,1:T(8,128)} collective-permute-done((f32[8192,128]{0,1:T(8,128)S(1)}, f32[8192,128]{0,1:T(8,128)}, u32[]{:S(2)}, u32[]{:S(2)}) %collective-permute-start.2) | collective-permute-done | bytes 4194336 | tf_op jit(solution)/shard_map/ppermute | solution.py:19
  500.5 15.4 %fusion.1 = f32[256,256]{0,1:T(8,128)} fusion(f32[8192,128]{0,1:T(8,128)} %copy-done.7, f32[8192,128]{0,1:T(8,128)} %collective-permute-done.2, pred[]{:T(512)S(6)} %eq.42), kind=kOutput, calls=%fused_computation.12 | convolution fusion | flops 6448742400 | bytes 8650753 | tf_op jit(solution)/shard_map/dot_general | solution.py:56
  516.0 47.7 %all-reduce.6.cloned.1.call-done = f32[256,256]{0,1:T(8,128)} async-done(((f32[256,256]{0,1:T(8,128)}), f32[256,256]{0,1:T(8,128)}) %all-reduce.6.cloned.1.call-update) | async-done | bytes 262160 | tf_op jit(solution)/shard_map/psum | solution.py:63
  563.7 2.7 gather_fusion.2
  566.4 1.6 convolution_add_fusion.1
  568.3 11.7 %cholesky.164 = f32[128,128]{1,0:T(8,128)S(1)} custom-call(f32[128,128]{1,0:T(8,128)S(1)} %cholesky.197), custom_call_target="Cholesky" | custom-call | tf_op jit(solution)/shard_map/jit(cholesky)/cholesky | solution.py:36
  580.0 9.8 %custom-call.21 = f32[1,128,128]{1,2,0:T(8,128)S(1)} custom-call(f32[1,128,128]{2,1,0:T(8,128)S(1)} %get-tuple-element.46), custom_call_target="InvertDiagBlocksLowerTriangular" | custom-call | tf_op jit(solution)/shard_map/jit(cholesky)/cholesky | solution.py:36
  589.8 0.2 constant_dynamic-update-slice_fusion
  590.1 0.3 convolution_subtract_fusion.4
  590.3 11.7 %cholesky.181 = f32[128,128]{1,0:T(8,128)S(1)} custom-call(f32[128,128]{1,0:T(8,128)S(1)} %convolution_subtract_fusion.4), custom_call_target="Cholesky" | custom-call | tf_op jit(solution)/shard_map/jit(cholesky)/cholesky | solution.py:36
  602.1 0.6 compare_reduce_fusion
  602.7 0.6 compare_reduce_fusion.1
  604.6 3.8 while.5
  604.6 0.6 fusion.74
  605.2 1.3 bitcast_dynamic-update-slice_fusion.5
  606.6 0.6 fusion.74
  607.1 1.3 bitcast_dynamic-update-slice_fusion.5
  608.5 19.8 %custom-call.22 = f32[2,128,128]{1,2,0:T(8,128)S(1)} custom-call(f32[2,128,128]{2,1,0:T(8,128)S(1)} %get-tuple-element.22), custom_call_target="InvertDiagBlocksLowerTriangular" | custom-call | tf_op jit(solution)/shard_map/jit(_cho_solve)/triangular_solve | solution.py:40
  628.3 0.8 fusion.13
  629.2 0.3 fusion.21
  629.5 0.3 convolution_subtract_fusion.1
  629.8 0.3 fusion.37
  630.1 0.3 fusion.36
  630.3 0.3 convolution_subtract_fusion
  630.7 0.3 fusion.35
  630.9 18.2 %fusion = f32[8192,128]{1,0:T(8,128)} fusion(f32[8192,128]{0,1:T(8,128)} %copy-done.7, f32[8192,128]{0,1:T(8,128)} %collective-permute-done.2, pred[]{:T(512)S(6)} %eq.42, s32[]{:T(128)S(6)} %select_n.63, f32[128,256]{1,0:T(8,128)S(1)} %fusion.35, f32[128,256]{1,0:T(8,128)S(1)} %fusion.36), kind=kOutput, calls=%fused_computation.11 | convolution fusion | flops 3227549696 | bytes 12845061 | tf_op jit(solution)/shard_map/dot_general | solution.py:67
  (45 shorter events, 0.9 us)
Async XLA Ops:
  6.5 1.6 copy-start
  6.5 225.5 %all-reduce.4.cloned.1.call-start = ((), (), s32[]{:S(2)}) async-start(), calls=%async_computation | async-start | bytes 524288 | tf_op jit(solution)/shard_map/psum | solution.py:63
  36.1 5.7 copy-start.3
  36.1 5.7 copy-start.5
  41.8 4.2 copy-start.4
  41.8 4.2 copy-start.6
  67.0 86.5 %collective-permute-start = (f32[8192,128]{0,1:T(8,128)}, f32[8192,128]{0,1:T(8,128)}, u32[]{:S(2)}, u32[]{:S(2)}) collective-permute-start(f32[8192,128]{0,1:T(8,128)} %broadcast_multiply_fusion), channel_id=1, source_target_pairs={{0,4},{4,0},{8,12},{12,8},{16,20},{20,16},{24,28},{28,24},{32,36},... | collective-permute-start | bytes 12582920 | tf_op jit(solution)/shard_map/ppermute | solution.py:19
  169.4 394.4 %all-reduce.6.cloned.1.call-start = ((), (), s32[]{:S(2)}) async-start(), calls=%async_computation.1 | async-start | bytes 524288 | tf_op jit(solution)/shard_map/psum | solution.py:63
  232.0 65.0 %copy-start.1 = (f32[256,256]{0,1:T(8,128)S(1)}, f32[256,256]{0,1:T(8,128)}, u32[]{:S(2)}) copy-start(f32[256,256]{0,1:T(8,128)} %all-reduce.4.cloned.1.call-done) | copy-start | bytes 786436
  308.3 98.6 %collective-permute-start.1 = (f32[8192,128]{0,1:T(8,128)S(1)}, f32[8192,128]{0,1:T(8,128)S(1)}, u32[]{:S(2)}, u32[]{:S(2)}) collective-permute-start(f32[8192,128]{0,1:T(8,128)S(1)} %fusion.2), channel_id=1, source_target_pairs={{252,0},{0,4},{4,8},{8,12},{12,16},{16,20},{20,24},{24,28},{28,32}... | collective-permute-start | bytes 12582920 | tf_op jit(solution)/shard_map/ppermute | solution.py:13
  406.9 1.9 copy-start.7
  408.8 91.7 %collective-permute-start.2 = (f32[8192,128]{0,1:T(8,128)S(1)}, f32[8192,128]{0,1:T(8,128)}, u32[]{:S(2)}, u32[]{:S(2)}) collective-permute-start(f32[8192,128]{0,1:T(8,128)S(1)} %collective-permute-done.1), channel_id=1, source_target_pairs={{0,4},{4,0},{8,12},{12,8},{16,20},{20,16},{24,28},{28,24},{32,36},... | collective-permute-start | bytes 12582920 | tf_op jit(solution)/shard_map/ppermute | solution.py:19
  563.7 64.6 %copy-start.2 = (f32[256,256]{0,1:T(8,128)S(1)}, f32[256,256]{0,1:T(8,128)}, u32[]{:S(2)}) copy-start(f32[256,256]{0,1:T(8,128)} %all-reduce.6.cloned.1.call-done) | copy-start | bytes 786436
Sparse Core Ops, SparseCore 0:
  169.5 62.4 all-reduce.3
  516.1 47.5 all-reduce.5
where the time goes:
time: 663 us; the launch traced here: 656 us
  waiting for transfers between devices  386 us (58%)
  other arithmetic  115 us (17%)
  matrix products  75.9 us (11%)
  local copies, waits for them, and re-layouts  49 us (7%)
  between operations  16.5 us (2%)
  blocking collectives  12.1 us (2%)
    ppermute x2, waiting for transfers between devices, from_partner(): return lax.ppermute(value, axis, pairs)  178 us
    psum x2, waiting for transfers between devices, slab_gram(): return lax.psum(gram_local, 'slab')  110 us
    ppermute x1, waiting for transfers between devices, from_behind(): return lax.ppermute(block, axis, route)  98.5 us
    another operation x14, other arithmetic, block_rotation(): factor = jnp.linalg.cholesky(symmetric)  69.2 us
    another operation x5, other arithmetic, block_rotation(): return jax.scipy.linalg.cho_solve((factor, True), numerator)  39.6 us
    gather x2, local copies, waits for them, and re-layouts, shards(): jacobian = jnp.take(clip_cache, clip_ids, axis=0) * dose_part + focus_part  33.6 us
    dot_general x2, matrix products, slab_gram(): lax.dot_general(pair_block, pair_block, (((0,), (0,)), ((), ())), precisi...  31.2 us
    dot_general x2, matrix products, product(): jnp.dot(left_side, right_side, precision=lax.Precision.HIGHEST, preferred...  27 us
  transfers between devices with their start and end apart: 5, of which 5 were waited for; matrix products, arithmetic and copies ran while one was open for 0% of the time, Pallas kernels for 0%

commit v1 on v0

--- a/solution.py
+++ b/solution.py
@@ -5,6 +5,11 @@
 
 ROUNDS = 2
 EPSILON = 1e-06
+
+
+def add_all(x, mesh_axis):
+    parts = lax.all_gather(x, mesh_axis)
+    return jnp.sum(parts, axis=0)
 
 
 def from_behind(block, axis, distance):
@@ -60,7 +65,7 @@
         precision=lax.Precision.HIGHEST,
         preferred_element_type=jnp.float32,
     )
-    return lax.psum(gram_local, "slab")
+    return add_all(gram_local, "slab")
 
 
 def product(left_side, right_side):

time: 663 us -> 619 us (0.934)
  waiting for transfers between devices: 386 us -> 341 us
    psum x2 -> x0, waiting for transfers between devices: 110 us -> none  [slab_gram(): return lax.psum(gram_local, 'slab')]
    all_gather x0 -> x2, waiting for transfers between devices: none -> 65.9 us  [add_all(): parts = lax.all_gather(x, mesh_axis)]
where the time goes in v1:
time: 619 us; the launch traced here: 612 us
  waiting for transfers between devices  341 us (55%)
  other arithmetic  118 us (19%)
  matrix products  74.3 us (12%)
  local copies, waits for them, and re-layouts  49.1 us (8%)
  between operations  16.4 us (3%)
  blocking collectives  12.1 us (2%)
    ppermute x2, waiting for transfers between devices, from_partner(): return lax.ppermute(value, axis, pairs)  177 us
    ppermute x1, waiting for transfers between devices, from_behind(): return lax.ppermute(block, axis, route)  97.6 us
    another operation x14, other arithmetic, block_rotation(): factor = jnp.linalg.cholesky(symmetric)  69.2 us
    all_gather x2, waiting for transfers between devices, add_all(): parts = lax.all_gather(x, mesh_axis)  65.9 us
    another operation x5, other arithmetic, block_rotation(): return jax.scipy.linalg.cho_solve((factor, True), numerator)  39.8 us
    gather x2, local copies, waits for them, and re-layouts, shards(): jacobian = jnp.take(clip_cache, clip_ids, axis=0) * dose_part + focus_part  33.6 us
    dot_general x2, matrix products, slab_gram(): lax.dot_general(pair_block, pair_block, (((0,), (0,)), ((), ())), precisi...  31.7 us
    dot_general x2, matrix products, product(): jnp.dot(left_side, right_side, precision=lax.Precision.HIGHEST, preferred...  27 us
  transfers between devices with their start and end apart: 5, of which 5 were waited for; matrix products, arithmetic and copies ran while one was open for 0% of the time, Pallas kernels for 0%

profile of v1, /device:TPU:1, one launch (start us, length us, event | category | flops | bytes accessed | tf_op | source)
XLA Modules:
  0.0 611.7 jit_solution(7579337594691621368)
XLA Ops:
  6.5 0.8 fusion.42
  7.4 0.8 compare_and_fusion
  8.2 28.0 %gather_fusion = f32[8192,128]{1,0:T(8,128)} fusion(f32[1024,128]{1,0:T(8,128)S(1)} %copy-done, s32[8192]{0:T(1024)S(1)} %fusion.42), kind=kCustom, calls=%fused_computation | custom fusion | bytes 8421376 | tf_op jit(solution)/shard_map/jit(_take)/gather | solution.py:83
  36.1 5.7 copy.29
  41.8 4.2 convolution_multiply_fusion
  46.0 4.2 multiply_reduce_fusion
  50.2 12.1 %psum.7 = f32[128]{0:T(128)S(1)} all-reduce(f32[128]{0:T(128)S(1)} %get-tuple-element.51), channel_id=1, replica_groups=mesh['panel'=64,'slab'=4] {'slab'}, use_global_device_ids=true, to_apply=%region_1.2 | all-reduce | flops 128 | bytes 1024 | tf_op jit(solution)/shard_map/psum | solution.py:84
  62.3 4.7 broadcast_multiply_fusion
  67.0 0.7 collective-permute-start
  67.7 85.9 %collective-permute-done = f32[8192,128]{0,1:T(8,128)} collective-permute-done((f32[8192,128]{0,1:T(8,128)}, f32[8192,128]{0,1:T(8,128)}, u32[]{:S(2)}, u32[]{:S(2)}) %collective-permute-start) | collective-permute-done | bytes 4194336 | tf_op jit(solution)/shard_map/ppermute | solution.py:24
  153.5 16.7 %fusion.3 = f32[256,256]{1,0:T(8,128)} fusion(f32[8192,128]{0,1:T(8,128)} %broadcast_multiply_fusion, f32[8192,128]{0,1:T(8,128)} %collective-permute-done, pred[]{:T(512)S(6)} %eq.42), kind=kOutput, calls=%fused_computation.14 | convolution fusion | flops 6448742400 | bytes 8650753 | tf_op jit(solution)/shard_map/dot_general | solution.py:61
  170.3 39.5 %all-gather.5.cloned.1.call-done = f32[1024,256]{1,0:T(8,128)} async-done(((f32[256,256]{1,0:T(8,128)}), f32[1024,256]{1,0:T(8,128)}) %all-gather.5.cloned.1.call-update) | async-done | bytes 1048592 | tf_op jit(solution)/shard_map/all_gather | solution.py:11
  209.9 1.3 reduce_sum.28
  211.3 2.5 gather_fusion.1
  213.9 0.6 convolution_add_fusion.2
  214.5 0.8 fusion.12
  215.5 11.7 %cholesky.130 = f32[128,128]{1,0:T(8,128)S(1)} custom-call(f32[128,128]{1,0:T(8,128)S(1)} %cholesky.194), custom_call_target="Cholesky" | custom-call | tf_op jit(solution)/shard_map/jit(cholesky)/cholesky | solution.py:41
  227.3 9.8 %custom-call.19 = f32[1,128,128]{1,2,0:T(8,128)S(1)} custom-call(f32[1,128,128]{2,1,0:T(8,128)S(1)} %get-tuple-element.50), custom_call_target="InvertDiagBlocksLowerTriangular" | custom-call | tf_op jit(solution)/shard_map/jit(cholesky)/cholesky | solution.py:41
  237.3 0.3 convolution_subtract_fusion.5
  237.6 11.7 %cholesky.147 = f32[128,128]{1,0:T(8,128)S(1)} custom-call(f32[128,128]{1,0:T(8,128)S(1)} %convolution_subtract_fusion.5), custom_call_target="Cholesky" | custom-call | tf_op jit(solution)/shard_map/jit(cholesky)/cholesky | solution.py:41
  249.4 0.7 compare_reduce_fusion.2
  250.0 0.6 compare_reduce_fusion.3
  252.0 3.9 while.4
  252.0 0.6 fusion.73
  252.6 1.3 bitcast_dynamic-update-slice_fusion.4
  254.0 0.6 fusion.73
  254.6 1.3 bitcast_dynamic-update-slice_fusion.4
  255.9 19.9 %custom-call.20 = f32[2,128,128]{1,2,0:T(8,128)S(1)} custom-call(f32[2,128,128]{2,1,0:T(8,128)S(1)} %get-tuple-element.21), custom_call_target="InvertDiagBlocksLowerTriangular" | custom-call | tf_op jit(solution)/shard_map/jit(_cho_solve)/triangular_solve | solution.py:45
  275.8 0.3 fusion.23
  276.1 0.3 convolution_subtract_fusion.3
  276.4 0.3 fusion.34
  276.7 0.3 fusion.33
  277.0 0.3 convolution_subtract_fusion.2
  277.3 0.3 fusion.32
  277.6 8.8 %fusion.2 = f32[8192,128]{0,1:T(8,128)S(1)} fusion(f32[8192,128]{0,1:T(8,128)} %broadcast_multiply_fusion, f32[8192,128]{0,1:T(8,128)} %collective-permute-done, pred[]{:T(512)S(6)} %eq.42, s32[]{:T(128)S(6)} %select_n.63, f32[128,256]{1,0:T(8,128)S(1)} %fusion.32, f32[128,256]{1,0:T(8,128)S(1)} %fusion.33), kind=kOutput, calls=%fused_computation.13 | convolution fusion | flops 3227549696 | bytes 12845061 | tf_op jit(solution)/shard_map/dot_general | solution.py:72
  286.4 0.4 collective-permute-start.1
  286.8 97.6 %collective-permute-done.1 = f32[8192,128]{0,1:T(8,128)S(1)} collective-permute-done((f32[8192,128]{0,1:T(8,128)S(1)}, f32[8192,128]{0,1:T(8,128)S(1)}, u32[]{:S(2)}, u32[]{:S(2)}) %collective-permute-start.1) | collective-permute-done | bytes 4194336 | tf_op jit(solution)/shard_map/ppermute | solution.py:18
  384.4 1.9 copy-done.5
  386.3 91.1 %collective-permute-done.2 = f32[8192,128]{0,1:T(8,128)} collective-permute-done((f32[8192,128]{0,1:T(8,128)S(1)}, f32[8192,128]{0,1:T(8,128)}, u32[]{:S(2)}, u32[]{:S(2)}) %collective-permute-start.2) | collective-permute-done | bytes 4194336 | tf_op jit(solution)/shard_map/ppermute | solution.py:24
  477.4 15.0 %fusion.1 = f32[256,256]{1,0:T(8,128)} fusion(f32[8192,128]{0,1:T(8,128)} %copy-done.5, f32[8192,128]{0,1:T(8,128)} %collective-permute-done.2, pred[]{:T(512)S(6)} %eq.42), kind=kOutput, calls=%fused_computation.12 | convolution fusion | flops 6448742400 | bytes 8650753 | tf_op jit(solution)/shard_map/dot_general | solution.py:61
  492.4 26.4 %all-gather.7.cloned.1.call-done = f32[1024,256]{1,0:T(8,128)} async-done(((f32[256,256]{1,0:T(8,128)}), f32[1024,256]{1,0:T(8,128)}) %all-gather.7.cloned.1.call-update) | async-done | bytes 1048592 | tf_op jit(solution)/shard_map/all_gather | solution.py:11
  518.8 1.3 reduce_sum.29
  520.3 2.7 gather_fusion.2
  523.0 0.6 convolution_add_fusion.1
  523.6 0.8 fusion.13
  524.7 11.7 %cholesky.164 = f32[128,128]{1,0:T(8,128)S(1)} custom-call(f32[128,128]{1,0:T(8,128)S(1)} %cholesky.197), custom_call_target="Cholesky" | custom-call | tf_op jit(solution)/shard_map/jit(cholesky)/cholesky | solution.py:41
  536.5 9.8 %custom-call.21 = f32[1,128,128]{1,2,0:T(8,128)S(1)} custom-call(f32[1,128,128]{2,1,0:T(8,128)S(1)} %get-tuple-element.46), custom_call_target="InvertDiagBlocksLowerTriangular" | custom-call | tf_op jit(solution)/shard_map/jit(cholesky)/cholesky | solution.py:41
  546.5 0.3 convolution_subtract_fusion.4
  546.8 11.7 %cholesky.181 = f32[128,128]{1,0:T(8,128)S(1)} custom-call(f32[128,128]{1,0:T(8,128)S(1)} %convolution_subtract_fusion.4), custom_call_target="Cholesky" | custom-call | tf_op jit(solution)/shard_map/jit(cholesky)/cholesky | solution.py:41
  558.5 0.6 compare_reduce_fusion
  559.1 0.6 compare_reduce_fusion.1
  561.0 3.8 while.5
  561.1 0.6 fusion.74
  561.6 1.3 bitcast_dynamic-update-slice_fusion.5
  563.0 0.6 fusion.74
  563.6 1.3 bitcast_dynamic-update-slice_fusion.5
  564.9 19.8 %custom-call.22 = f32[2,128,128]{1,2,0:T(8,128)S(1)} custom-call(f32[2,128,128]{2,1,0:T(8,128)S(1)} %get-tuple-element.22), custom_call_target="InvertDiagBlocksLowerTriangular" | custom-call | tf_op jit(solution)/shard_map/jit(_cho_solve)/triangular_solve | solution.py:45
  584.7 0.3 fusion.21
  585.1 0.3 convolution_subtract_fusion.1
  585.3 0.3 fusion.37
  585.6 0.3 fusion.36
  585.9 0.3 convolution_subtract_fusion
  586.2 0.3 fusion.35
  586.5 18.2 %fusion = f32[8192,128]{1,0:T(8,128)} fusion(f32[8192,128]{0,1:T(8,128)} %copy-done.5, f32[8192,128]{0,1:T(8,128)} %collective-permute-done.2, pred[]{:T(512)S(6)} %eq.42, s32[]{:T(128)S(6)} %select_n.63, f32[128,256]{1,0:T(8,128)S(1)} %fusion.35, f32[128,256]{1,0:T(8,128)S(1)} %fusion.36), kind=kOutput, calls=%fused_computation.11 | convolution fusion | flops 3227549696 | bytes 12845061 | tf_op jit(solution)/shard_map/dot_general | solution.py:72
  (45 shorter events, 1.5 us)
Async XLA Ops:
  6.5 1.6 copy-start
  6.5 203.3 %all-gather.5.cloned.1.call-start = ((), (), s32[]{:S(2)}) async-start(), calls=%async_computation | async-start | bytes 1310720 | tf_op jit(solution)/shard_map/all_gather | solution.py:11
  36.1 5.7 copy-start.1
  36.1 5.7 copy-start.3
  41.8 4.2 copy-start.2
  41.8 4.2 copy-start.4
  67.0 86.5 %collective-permute-start = (f32[8192,128]{0,1:T(8,128)}, f32[8192,128]{0,1:T(8,128)}, u32[]{:S(2)}, u32[]{:S(2)}) collective-permute-start(f32[8192,128]{0,1:T(8,128)} %broadcast_multiply_fusion), channel_id=1, source_target_pairs={{0,4},{4,0},{8,12},{12,8},{16,20},{20,16},{24,28},{28,24},{32,36},... | collective-permute-start | bytes 12582920 | tf_op jit(solution)/shard_map/ppermute | solution.py:24
  170.3 348.5 %all-gather.7.cloned.1.call-start = ((), (), s32[]{:S(2)}) async-start(), calls=%async_computation.1 | async-start | bytes 1310720 | tf_op jit(solution)/shard_map/all_gather | solution.py:11
  286.4 98.0 %collective-permute-start.1 = (f32[8192,128]{0,1:T(8,128)S(1)}, f32[8192,128]{0,1:T(8,128)S(1)}, u32[]{:S(2)}, u32[]{:S(2)}) collective-permute-start(f32[8192,128]{0,1:T(8,128)S(1)} %fusion.2), channel_id=1, source_target_pairs={{252,0},{0,4},{4,8},{8,12},{12,16},{16,20},{20,24},{24,28},{28,32}... | collective-permute-start | bytes 12582920 | tf_op jit(solution)/shard_map/ppermute | solution.py:18
  384.4 1.9 copy-start.5
  386.3 91.1 %collective-permute-start.2 = (f32[8192,128]{0,1:T(8,128)S(1)}, f32[8192,128]{0,1:T(8,128)}, u32[]{:S(2)}, u32[]{:S(2)}) collective-permute-start(f32[8192,128]{0,1:T(8,128)S(1)} %collective-permute-done.1), channel_id=1, source_target_pairs={{0,4},{4,0},{8,12},{12,8},{16,20},{20,16},{24,28},{28,24},{32,36},... | collective-permute-start | bytes 12582920 | tf_op jit(solution)/shard_map/ppermute | solution.py:24
Sparse Core Ops, SparseCore 0:
  170.4 39.4 all-gather.4
  492.5 26.2 all-gather.6
